TPU v7x, 32 devices: a whole 2x2x4 slice. The times are simulated.
32 devices in a mesh: row: 4 (over y, x), col: 8 (over z, core).
Axes of the slice: x: 2, y: 2, z: 4, core: 2. Of those that a mesh axis runs over, the one named last changes fastest.
Arguments:
- amplitudes: float32 [8, 8, 256, 256], P('row', 'col'), may hold values from -6 to 6
- coulomb: bfloat16 [8, 8, 256, 256], P('row'), may hold values from -6 to 6
- inner_list: int32 [8, 8, 8], P('row', 'col'), may hold values from 0 to 7, as said below
- inner_count: int32 [8, 8], P('row', 'col'), may hold values from 4 to 8
- reader_list: int32 [8, 8, 8], P('row'), may hold values from 0 to 7, as said below
- reader_count: int32 [8, 8], P('row'), may hold values from 4 to 8
- virtual_energy: float32 [256], replicated, may hold values from 0.5 to 2.5
- occupied_energy: float32 [8], replicated, may hold values from -1.5 to -0.3
Outputs:
- new_amplitudes: float32 [8, 8, 256, 256], P('row', 'col')
Inputs may be any that keep to these rules, and one draw needn't show every extreme that they name: `inner_list`: for each pair block the 8 entries are distinct orbitals; only the first inner_count of them are used. `reader_list`: for each pair block the 8 entries are distinct orbitals; only the first reader_count of them are used.
All inputs are finite; a program needn't handle non-finite values.
Results may differ from a plain program's by a relative error of at most 0.0015.
Values may be sent and summed in bfloat16 or wider, within the bound.
No kernel may reach another device: no remote copies, remote signals or barrier semaphores. Data moves between devices by JAX's collectives and lax.ppermute only.
A program may use at most 64 MiB of HBM per device.

v0:
```python
import functools

import jax
import jax.numpy as jnp
from jax import lax
from jax.experimental import pallas as pl
from jax.experimental.pallas import tpu as pltpu
from jax.sharding import PartitionSpec as P

ITERS = 2


damping = 0.5
coupling = 0.03125
ANY = pl.BlockSpec(memory_space=pl.ANY)
SMEM = pl.BlockSpec(memory_space=pltpu.SMEM)
VMEM = pl.BlockSpec(memory_space=pltpu.VMEM)
VMEM_BYTES = 32 * 1024 * 1024


def call(body, out_shape, in_specs, flops, moved, *operands):
    single = isinstance(out_shape, jax.ShapeDtypeStruct)
    return pl.pallas_call(
        body,
        out_shape=out_shape,
        in_specs=in_specs,
        out_specs=VMEM if single else (VMEM,) * len(out_shape),
        compiler_params=pltpu.CompilerParams(vmem_limit_bytes=VMEM_BYTES),
        cost_estimate=pl.CostEstimate(flops=flops, bytes_accessed=moved, transcendentals=0),
    )(*operands)


def prologue_body(meta, occupied, k_ref, virt_row, virt_col, kept_ref, own_ref, inverse_ref):
    orb_rows, _, virt, _ = k_ref.shape
    my_row = meta[2 * orb_rows, 0]
    my_col = meta[2 * orb_rows, 1]
    for step in range(kept_ref.shape[0]):
        for t in range(orb_rows):
            orbital = (my_row ^ step) * orb_rows + t
            for i in range(orb_rows):
                block = k_ref[i, orbital]
                keep = jnp.where(meta[i, orbital] > 0, block, jnp.zeros_like(block))
                kept_ref[step, i * virt : (i + 1) * virt, t * virt : (t + 1) * virt] = keep
    virt_pair = virt_col[...] + virt_row[...]
    for i in range(orb_rows):
        own_ref[i] = k_ref[i, my_col]
        inverse_ref[i] = 1.0 / (virt_pair - occupied[0, my_row * orb_rows + i] - occupied[0, my_col])


def prologue(rows, meta, coulomb, virtual_energy, occupied_energy):
    orb_rows, count, virt, _ = coulomb.shape
    shape = (
        jax.ShapeDtypeStruct((rows, orb_rows * virt, orb_rows * virt), jnp.bfloat16),
        jax.ShapeDtypeStruct((orb_rows, virt, virt), jnp.bfloat16),
        jax.ShapeDtypeStruct((orb_rows, virt, virt), jnp.float32),
    )
    return call(
        prologue_body, shape, [SMEM, SMEM, VMEM, VMEM, VMEM], 0, 4 * orb_rows * count * virt**2,
        meta, occupied_energy[None], coulomb, virtual_energy[None], virtual_energy[:, None],
    )


def piece_blocks(refs, rows):
    found, refs, size = [], list(refs), refs[0].shape[0]
    for step in range(rows):
        blocks = []
        while len(blocks) < size:
            ref = refs.pop(0)
            blocks += [(ref, at) for at in range(ref.shape[0])]
        found.append(blocks)
    return found


def coupled_body(rows, k_ref, *refs):
    out_ref = refs[-1]
    orb_rows, virt, _ = out_ref.shape
    blocks = piece_blocks(refs[:-1], rows)
    total = None
    for step in range(rows):
        for t in range(orb_rows):
            ref, at = blocks[step][t]
            left = k_ref[step, :, t * virt : (t + 1) * virt]
            part = jnp.dot(left, ref[at], preferred_element_type=jnp.float32)
            total = part if total is None else total + part
    out_ref[...] = total.astype(out_ref.dtype).reshape(out_ref.shape)


def coupled_blocks(rows, kept, pieces):
    orb_rows, virt, _ = pieces[0].shape
    count = rows * orb_rows
    shape = jax.ShapeDtypeStruct((orb_rows, virt, virt), jnp.bfloat16)
    body = functools.partial(coupled_body, rows)
    flops, moved = 2 * orb_rows * count * virt**3, 2 * (orb_rows + 1) * count * virt**2
    return call(body, shape, [VMEM] * (1 + len(pieces)), flops, moved, kept, *pieces)


def placed(meta, ref, hops, out_ref):
    orb_rows = ref.shape[0]
    halves = out_ref.shape[0] // orb_rows
    for hop in hops:
        spot = meta[2 * orb_rows, 1] // 2 + hop

        @pl.when(jnp.logical_and(spot >= 0, spot < halves))
        def _():
            out_ref[pl.ds(spot * orb_rows, orb_rows)] = ref[...]


def column_body(places, meta, crossing_ref, *refs):
    out_ref, same_ref, other_ref = refs[-3:]
    side = meta[2 * crossing_ref.shape[0], 1] % 2
    for ref, hops in zip(refs, places):
        placed(meta, ref, hops, out_ref)
    same_ref[...] = crossing_ref[side]
    other_ref[...] = crossing_ref[1 - side]


def whole_column(meta, halves, pieces, places, crossing, others):
    orb_rows, virt, _ = pieces[0].shape
    block = jax.ShapeDtypeStruct((virt, virt), jnp.bfloat16)
    shape = (jax.ShapeDtypeStruct((orb_rows * halves, virt, virt), jnp.bfloat16), block, block)
    operands = [crossing, *pieces, *others]
    moved = 4 * orb_rows * (halves + 1) * virt**2
    body = functools.partial(column_body, places)
    return call(body, shape, [SMEM] + [VMEM] * len(operands), 0, moved, meta, *operands)


def masked_pair(meta, orbital, blocks):
    orb_rows = len(blocks)
    kept = [jnp.where(meta[orb_rows + i, orbital] > 0, block, jnp.zeros_like(block)) for i, block in enumerate(blocks)]
    return jnp.concatenate(kept, axis=0)


def turned(block):
    return jnp.transpose(block.astype(jnp.float32), (1, 0))


def first_body(rows, meta, own_ref, other_ref, *refs):
    state_ref, coulomb_ref, inverse_ref, out_ref = refs[-4:]
    orb_rows = out_ref.shape[0]
    blocks = piece_blocks(refs[:-4], rows)
    my_row, side = meta[2 * orb_rows, 0], meta[2 * orb_rows, 1] % 2
    total = None
    for step in range(rows):
        at = my_row ^ step
        for t in range(orb_rows):
            left = [
                jnp.where(side == t, own_ref[at * orb_rows + i], other_ref[at * orb_rows + i]) for i in range(orb_rows)
            ]
            ref, place = blocks[step][t]
            left = masked_pair(meta, at * orb_rows + t, left)
            part = jnp.dot(left, ref[place], preferred_element_type=jnp.float32)
            total = part if total is None else total + part
    linear = coulomb_ref[...].astype(jnp.float32) + coupling * refs[0][...].astype(jnp.float32)
    residual = linear + coupling * coupling * total.reshape(out_ref.shape)
    out_ref[...] = damping * state_ref[...] - residual * inverse_ref[...]


def second_body(meta, same_ref, other_ref, part_ref, inverse_ref, out_ref, half_ref):
    side = meta[2 * out_ref.shape[0], 1] % 2
    for ref, at in ((same_ref, side), (other_ref, 1 - side)):
        state = part_ref[at] - coupling * turned(ref[...]) * inverse_ref[at]
        out_ref[at] = state
        half_ref[at] = state.astype(half_ref.dtype)


def first_update(rows, meta, own, other, c_pieces, state, coulomb_own, inverse):
    orb_rows, virt, _ = state.shape
    shape = jax.ShapeDtypeStruct(state.shape, jnp.float32)
    flops, moved = 2 * orb_rows**2 * rows * virt**3, 4 * (orb_rows + 1) * orb_rows * rows * virt**2
    return call(
        functools.partial(first_body, rows), shape, [SMEM] + [VMEM] * (len(c_pieces) + 5), flops, moved,
        meta, own, other, *c_pieces, state, coulomb_own, inverse,
    )


def second_update(meta, same, other, part, inverse):
    shape = (jax.ShapeDtypeStruct(part.shape, jnp.float32), jax.ShapeDtypeStruct(part.shape, jnp.bfloat16))
    return call(second_body, shape, [SMEM] + [VMEM] * 4, 0, 16 * part.size, meta, same, other, part, inverse)


def on_device(
    rows,
    cols,
    amplitudes,
    coulomb,
    inner_list,
    inner_count,
    reader_list,
    reader_count,
    virtual_energy,
    occupied_energy,
):
    orb_rows, orb_cols, virt, _ = amplitudes.shape
    count = coulomb.shape[1]
    slots = inner_list.shape[2]
    assert orb_cols == 1 and count == cols == rows * orb_rows and orb_rows == 2
    halves = cols // 2
    my_row = lax.axis_index("row")
    my_col = lax.axis_index("col")

    def from_row(x, step):
        return lax.ppermute(x, "row", [(r ^ step, r) for r in range(rows)])

    def row_gathered(x, halved):
        near = from_row(x, 1)
        pieces = [x, near]
        for step in range(2, rows, 2):
            piece = from_row(x, step)
            if halved:
                pieces += [piece, from_row(piece[0:1], 1), from_row(near[1:2], step)]
            else:
                pieces += [piece, from_row(near, step)]
        return pieces

    def swapped(x):
        return lax.ppermute(x, "col", [(c ^ 1, c) for c in range(cols)])

    def along(x, hops):
        return lax.ppermute(
            x, "col", [(2 * at + k, 2 * (at + hop) + k) for at, hop in hops for k in range(2)]
        )

    def relayed(x):
        pieces, places = [x], [(0,)]
        up = down = x
        for stage in range(1, halves):
            ups = [(at, 1) for at in range(stage - 1, halves - 1)]
            downs = [(at, -1) for at in range(1, halves - stage + 1)]
            if stage - 1 > halves - stage:
                up = down = along(jnp.where(my_col // 2 >= stage - 1, up, down), ups + downs)
                pieces.append(up)
                places.append((-stage, stage))
            else:
                up, down = along(up, ups), along(down, downs)
                pieces += [up, down]
                places += [(-stage,), (stage,)]
        return pieces, tuple(places)

    def crossing(x, place, flip=0):
        pairs = []
        for r in range(rows):
            for c in range(cols):
                to_r, to_z = place(r, c // 2)
                pairs.append((r * cols + c, to_r * cols + 2 * to_z + (c % 2 ^ flip)))
        return lax.ppermute(x, ("row", "col"), pairs)

    def high_parts(r, z):
        return z - z % 2 + r % 2, r - r % 2 + z % 2

    def last_bits(r, z):
        return r - r % 2 + z % 2, z - z % 2 + r % 2

    state = amplitudes[:, 0]
    half = state.astype(jnp.bfloat16)

    slot_iota = jnp.arange(slots, dtype=jnp.int32)
    orbital_iota = jnp.arange(count, dtype=jnp.int32)

    def used(lists, counts):
        live = slot_iota[None] < counts[:, None]
        hit = (lists[:, :, None] == orbital_iota) & live[:, :, None]
        return jnp.any(hit, axis=1).astype(jnp.int32)

    inner_used = used(inner_list[:, 0], inner_count[:, 0])
    reader_used = used(
        lax.dynamic_index_in_dim(reader_list, my_col, 1, False), lax.dynamic_index_in_dim(reader_count, my_col, 1, False)
    )
    place = jnp.where(orbital_iota == 0, my_row, my_col).astype(jnp.int32)
    meta = jnp.concatenate([inner_used, reader_used, place[None]], axis=0)

    kept, coulomb_own, inverse = prologue(rows, meta, coulomb, virtual_energy, occupied_energy)

    for sweep_index in range(ITERS):
        a_pieces = row_gathered(half, True)
        column, places = relayed(half)
        coupled = coupled_blocks(rows, kept, a_pieces)
        c_pieces = row_gathered(coupled, False)
        half_way = crossing(coupled, high_parts)
        own, same, other = whole_column(meta, halves, column, places, half_way, c_pieces[1:3])
        same, other = crossing(same, last_bits), crossing(other, last_bits, 1)
        part = first_update(rows, meta, own, swapped(own), c_pieces, state, coulomb_own, inverse)
        state, half = second_update(meta, same, other, part, inverse)
    return state[:, None]


def solution(mesh):
    return jax.shard_map(
        functools.partial(on_device, mesh.shape["row"], mesh.shape["col"]),
        mesh=mesh,
        in_specs=(
            P("row", "col", None, None),
            P("row", None, None, None),
            P("row", "col", None),
            P("row", "col"),
            P("row", None, None),
            P("row", None),
            P(),
            P(),
        ),
        out_specs=P("row", "col", None, None),
        check_vma=False,
    )
```

profile of v0, /device:TPU:7, one launch (start us, length us, event | category | flops | bytes accessed | tf_op | source)
XLA Modules:
  0.0 109.6 jit_solution(5068053190894253895)
XLA Ops:
  1.1 3.2 %collective-permute-start.5 = (bf16[2,256,256]{2,1,0:T(8,128)(2,1)S(1)}, bf16[2,256,256]{2,1,0:T(8,128)(2,1)S(1)}, u32[]{:S(2)}, u32[]{:S(2)}) collective-permute-start(bf16[2,256,256]{2,1,0:T(8,128)(2,1)S(1)} %bitcast_convert_fusion.refs_0_), channel_id=1, source_target_pairs={{0,2},{1,3},{2,4},{3,5},{4,6},{5,7},{8,10},{9,11},{10,12},{11,13},... | collective-permute-start | bytes 786440 | tf_op jit(solution)/shard_map/ppermute | solution.py:219
  4.3 1.3 %collective-permute-start.6 = (bf16[2,256,256]{2,1,0:T(8,128)(2,1)S(1)}, bf16[2,256,256]{2,1,0:T(8,128)(2,1)S(1)}, u32[]{:S(2)}, u32[]{:S(2)}) collective-permute-start(bf16[2,256,256]{2,1,0:T(8,128)(2,1)S(1)} %bitcast_convert_fusion.refs_0_), channel_id=1, source_target_pairs={{2,0},{3,1},{4,2},{5,3},{6,4},{7,5},{10,8},{11,9},{12,10},{13,11},... | collective-permute-start | bytes 786440 | tf_op jit(solution)/shard_map/ppermute | solution.py:219
  8.7 3.8 %collective-permute-done.1.refs_2_ = bf16[2,256,256]{2,1,0:T(8,128)(2,1)S(1)} collective-permute-done((bf16[2,256,256]{2,1,0:T(8,128)(2,1)S(1)}, bf16[2,256,256]{2,1,0:T(8,128)(2,1)S(1)}, u32[]{:S(2)}, u32[]{:S(2)}) %collective-permute-start.1) | collective-permute-done | bytes 262176 | tf_op jit(solution)/shard_map/ppermute | solution.py:202
  14.5 1.3 %collective-permute-start.8 = (bf16[2,256,256]{2,1,0:T(8,128)(2,1)S(1)}, bf16[2,256,256]{2,1,0:T(8,128)(2,1)S(1)}, u32[]{:S(2)}, u32[]{:S(2)}) collective-permute-start(bf16[2,256,256]{2,1,0:T(8,128)(2,1)S(1)} %collective-permute-done.6.refs_2_), channel_id=1, source_target_pairs={{2,0},{3,1},{4,2},{5,3},{10,8},{11,9},{12,10},{13,11},{18,16},{19,... | collective-permute-start | bytes 786440 | tf_op jit(solution)/shard_map/ppermute | solution.py:219
  16.7 1.6 %copy-done.1 = bf16[2,8,256,256]{3,2,1,0:T(8,128)(2,1)S(1)} copy-done((bf16[2,8,256,256]{3,2,1,0:T(8,128)(2,1)S(1)}, bf16[2,8,256,256]{3,2,1,0:T(8,128)(2,1)}, u32[]{:S(2)}) %copy-start.1) | copy-done | bytes 2097176
  23.2 8.0 %collective-permute-start.4 = (bf16[2,256,256]{2,1,0:T(8,128)(2,1)S(1)}, bf16[2,256,256]{2,1,0:T(8,128)(2,1)S(1)}, u32[]{:S(2)}, u32[]{:S(2)}) collective-permute-start(bf16[2,256,256]{2,1,0:T(8,128)(2,1)S(1)} %shard_map.86.refs_0_), channel_id=1, source_target_pairs={{0,0},{1,1},{2,2},{3,3},{4,16},{5,17},{6,18},{7,19},{8,8},{9,9},{1... | collective-permute-start | bytes 786440 | tf_op jit(solution)/shard_map/ppermute | solution.py:245
  31.2 1.3 %collective-permute-start.9 = (bf16[2,256,256]{2,1,0:T(8,128)(2,1)S(1)}, bf16[2,256,256]{2,1,0:T(8,128)(2,1)S(1)}, u32[]{:S(2)}, u32[]{:S(2)}) collective-permute-start(bf16[2,256,256]{2,1,0:T(8,128)(2,1)S(1)} %broadcast_select_fusion.1), channel_id=1, source_target_pairs={{4,6},{5,7},{2,0},{3,1},{12,14},{13,15},{10,8},{11,9},{20,22},{21,... | collective-permute-start | bytes 786440 | tf_op jit(solution)/shard_map/ppermute | solution.py:219
  32.5 9.2 %collective-permute-done.4.crossing_ref = bf16[2,256,256]{2,1,0:T(8,128)(2,1)S(1)} collective-permute-done((bf16[2,256,256]{2,1,0:T(8,128)(2,1)S(1)}, bf16[2,256,256]{2,1,0:T(8,128)(2,1)S(1)}, u32[]{:S(2)}, u32[]{:S(2)}) %collective-permute-start.4) | collective-permute-done | bytes 262176 | tf_op jit(solution)/shard_map/ppermute | solution.py:245
  42.5 2.4 %collective-permute-start.14 = (bf16[8,256,256]{2,1,0:T(8,128)(2,1)S(1)}, bf16[8,256,256]{2,1,0:T(8,128)(2,1)S(1)}, u32[]{:S(2)}, u32[]{:S(2)}) collective-permute-start(bf16[8,256,256]{2,1,0:T(8,128)(2,1)S(1)} %get-tuple-element.20.own_ref), channel_id=1, source_target_pairs={{1,0},{0,1},{3,2},{2,3},{5,4},{4,5},{7,6},{6,7},{9,8},{8,9},{11,10... | collective-permute-start | bytes 3145736 | tf_op jit(solution)/shard_map/ppermute | solution.py:216
  45.0 1.9 %collective-permute-start.12 = (bf16[256,256]{1,0:T(8,128)(2,1)S(1)}, bf16[256,256]{1,0:T(8,128)(2,1)S(1)}, u32[]{:S(2)}, u32[]{:S(2)}) collective-permute-start(bf16[256,256]{1,0:T(8,128)(2,1)S(1)} %get-tuple-element.18), channel_id=1, source_target_pairs={{0,0},{1,1},{2,8},{3,9},{4,4},{5,5},{6,12},{7,13},{8,2},{9,3},{10,... | collective-permute-start | bytes 393224 | tf_op jit(solution)/shard_map/ppermute | solution.py:245
  46.9 2.7 %collective-permute-start.13 = (bf16[256,256]{1,0:T(8,128)(2,1)S(1)}, bf16[256,256]{1,0:T(8,128)(2,1)S(1)}, u32[]{:S(2)}, u32[]{:S(2)}) collective-permute-start(bf16[256,256]{1,0:T(8,128)(2,1)S(1)} %get-tuple-element.19), channel_id=1, source_target_pairs={{0,1},{1,0},{2,9},{3,8},{4,5},{5,4},{6,13},{7,12},{8,3},{9,2},{10,... | collective-permute-start | bytes 393224 | tf_op jit(solution)/shard_map/ppermute | solution.py:245
  49.6 3.3 %collective-permute-done.15.refs_3_ = bf16[2,256,256]{2,1,0:T(8,128)(2,1)S(1)} collective-permute-done((bf16[2,256,256]{2,1,0:T(8,128)(2,1)S(1)}, bf16[2,256,256]{2,1,0:T(8,128)(2,1)S(1)}, u32[]{:S(2)}, u32[]{:S(2)}) %collective-permute-start.15) | collective-permute-done | bytes 262176 | tf_op jit(solution)/shard_map/ppermute | solution.py:202
  52.9 1.4 %shard_map.88.part_ref = f32[2,256,256]{2,1,0:T(8,128)S(1)} custom-call(s32[5,8]{1,0:T(8,128)S(1)} %pad_add_fusion.meta, bf16[8,256,256]{2,1,0:T(8,128)(2,1)S(1)} %get-tuple-element.20.own_ref, bf16[8,256,256]{2,1,0:T(8,128)(2,1)S(1)} %collective-permute-done.14.other_ref, bf16[2,256,256]{2,1,0:T(8,128)(2,1)S(1)} %shard_map.86.refs_0_, ...), custom_call_target="tpu_custom_call" | custom-call | flops 536870912 | bytes 6291456 | tf_op jit(solution)/shard_map/pallas_call | solution.py:23
  54.3 1.5 %collective-permute-done.13.other_ref = bf16[256,256]{1,0:T(8,128)(2,1)S(1)} collective-permute-done((bf16[256,256]{1,0:T(8,128)(2,1)S(1)}, bf16[256,256]{1,0:T(8,128)(2,1)S(1)}, u32[]{:S(2)}, u32[]{:S(2)}) %collective-permute-start.13) | collective-permute-done | bytes 131104 | tf_op jit(solution)/shard_map/ppermute | solution.py:245
  56.6 1.3 %collective-permute-start.21 = (bf16[2,256,256]{2,1,0:T(8,128)(2,1)S(1)}, bf16[2,256,256]{2,1,0:T(8,128)(2,1)S(1)}, u32[]{:S(2)}, u32[]{:S(2)}) collective-permute-start(bf16[2,256,256]{2,1,0:T(8,128)(2,1)S(1)} %get-tuple-element.23.refs_0_), channel_id=1, source_target_pairs={{0,2},{1,3},{2,4},{3,5},{4,6},{5,7},{8,10},{9,11},{10,12},{11,13},... | collective-permute-start | bytes 786440 | tf_op jit(solution)/shard_map/ppermute | solution.py:219
  57.9 1.3 %collective-permute-start.22 = (bf16[2,256,256]{2,1,0:T(8,128)(2,1)S(1)}, bf16[2,256,256]{2,1,0:T(8,128)(2,1)S(1)}, u32[]{:S(2)}, u32[]{:S(2)}) collective-permute-start(bf16[2,256,256]{2,1,0:T(8,128)(2,1)S(1)} %get-tuple-element.23.refs_0_), channel_id=1, source_target_pairs={{2,0},{3,1},{4,2},{5,3},{6,4},{7,5},{10,8},{11,9},{12,10},{13,11},... | collective-permute-start | bytes 786440 | tf_op jit(solution)/shard_map/ppermute | solution.py:219
  59.2 1.5 %collective-permute-start.17 = (bf16[2,256,256]{2,1,0:T(8,128)(2,1)S(1)}, bf16[2,256,256]{2,1,0:T(8,128)(2,1)S(1)}, u32[]{:S(2)}, u32[]{:S(2)}) collective-permute-start(bf16[2,256,256]{2,1,0:T(8,128)(2,1)S(1)} %get-tuple-element.23.refs_0_), channel_id=1, source_target_pairs={{16,0},{24,8},{0,16},{8,24},{17,1},{25,9},{1,17},{9,25},{18,2},{26... | collective-permute-start | bytes 786440 | tf_op jit(solution)/shard_map/ppermute | solution.py:202
  62.0 1.7 %collective-permute-done.21.refs_1_ = bf16[2,256,256]{2,1,0:T(8,128)(2,1)S(1)} collective-permute-done((bf16[2,256,256]{2,1,0:T(8,128)(2,1)S(1)}, bf16[2,256,256]{2,1,0:T(8,128)(2,1)S(1)}, u32[]{:S(2)}, u32[]{:S(2)}) %collective-permute-start.21) | collective-permute-done | bytes 262176 | tf_op jit(solution)/shard_map/ppermute | solution.py:219
  64.3 3.3 %collective-permute-done.22.refs_2_ = bf16[2,256,256]{2,1,0:T(8,128)(2,1)S(1)} collective-permute-done((bf16[2,256,256]{2,1,0:T(8,128)(2,1)S(1)}, bf16[2,256,256]{2,1,0:T(8,128)(2,1)S(1)}, u32[]{:S(2)}, u32[]{:S(2)}) %collective-permute-start.22) | collective-permute-done | bytes 262176 | tf_op jit(solution)/shard_map/ppermute | solution.py:219
  69.3 1.8 %collective-permute-start.19 = (bf16[1,256,256]{2,1,0:T(8,128)(2,1)S(1)}, bf16[1,256,256]{2,1,0:T(8,128)(2,1)S(1)}, u32[]{:S(2)}, u32[]{:S(2)}) collective-permute-start(bf16[1,256,256]{2,1,0:T(8,128)(2,1)S(1)} %slice.19), channel_id=1, source_target_pairs={{16,0},{24,8},{0,16},{8,24},{17,1},{25,9},{1,17},{9,25},{18,2},{26... | collective-permute-start | bytes 393224 | tf_op jit(solution)/shard_map/ppermute | solution.py:202
  71.2 1.6 %collective-permute-done.18.refs_3_ = bf16[1,256,256]{2,1,0:T(8,128)(2,1)S(1)} collective-permute-done((bf16[1,256,256]{2,1,0:T(8,128)(2,1)S(1)}, bf16[1,256,256]{2,1,0:T(8,128)(2,1)S(1)}, u32[]{:S(2)}, u32[]{:S(2)}) %collective-permute-start.18) | collective-permute-done | bytes 131104 | tf_op jit(solution)/shard_map/ppermute | solution.py:202
  74.5 5.6 %collective-permute-start.20 = (bf16[2,256,256]{2,1,0:T(8,128)(2,1)S(1)}, bf16[2,256,256]{2,1,0:T(8,128)(2,1)S(1)}, u32[]{:S(2)}, u32[]{:S(2)}) collective-permute-start(bf16[2,256,256]{2,1,0:T(8,128)(2,1)S(1)} %shard_map.90.refs_0_), channel_id=1, source_target_pairs={{0,0},{1,1},{2,2},{3,3},{4,16},{5,17},{6,18},{7,19},{8,8},{9,9},{1... | collective-permute-start | bytes 786440 | tf_op jit(solution)/shard_map/ppermute | solution.py:245
  80.4 1.3 %collective-permute-start.25 = (bf16[2,256,256]{2,1,0:T(8,128)(2,1)S(1)}, bf16[2,256,256]{2,1,0:T(8,128)(2,1)S(1)}, u32[]{:S(2)}, u32[]{:S(2)}) collective-permute-start(bf16[2,256,256]{2,1,0:T(8,128)(2,1)S(1)} %broadcast_select_fusion), channel_id=1, source_target_pairs={{4,6},{5,7},{2,0},{3,1},{12,14},{13,15},{10,8},{11,9},{20,22},{21,... | collective-permute-start | bytes 786440 | tf_op jit(solution)/shard_map/ppermute | solution.py:219
  81.7 9.0 %collective-permute-done.20.crossing_ref = bf16[2,256,256]{2,1,0:T(8,128)(2,1)S(1)} collective-permute-done((bf16[2,256,256]{2,1,0:T(8,128)(2,1)S(1)}, bf16[2,256,256]{2,1,0:T(8,128)(2,1)S(1)}, u32[]{:S(2)}, u32[]{:S(2)}) %collective-permute-start.20) | collective-permute-done | bytes 262176 | tf_op jit(solution)/shard_map/ppermute | solution.py:245
  91.5 3.2 %collective-permute-start.30 = (bf16[8,256,256]{2,1,0:T(8,128)(2,1)S(1)}, bf16[8,256,256]{2,1,0:T(8,128)(2,1)S(1)}, u32[]{:S(2)}, u32[]{:S(2)}) collective-permute-start(bf16[8,256,256]{2,1,0:T(8,128)(2,1)S(1)} %get-tuple-element.26.own_ref), channel_id=1, source_target_pairs={{1,0},{0,1},{3,2},{2,3},{5,4},{4,5},{7,6},{6,7},{9,8},{8,9},{11,10... | collective-permute-start | bytes 3145736 | tf_op jit(solution)/shard_map/ppermute | solution.py:216
  94.7 2.5 %collective-permute-start.31 = (bf16[2,256,256]{2,1,0:T(8,128)(2,1)S(1)}, bf16[2,256,256]{2,1,0:T(8,128)(2,1)S(1)}, u32[]{:S(2)}, u32[]{:S(2)}) collective-permute-start(bf16[2,256,256]{2,1,0:T(8,128)(2,1)S(1)} %collective-permute-done.26.refs_6_.refs_1_), channel_id=1, source_target_pairs={{16,0},{24,8},{0,16},{8,24},{17,1},{25,9},{1,17},{9,25},{18,2},{26... | collective-permute-start | bytes 786440 | tf_op jit(solution)/shard_map/ppermute | solution.py:202
  97.2 2.0 %collective-permute-start.28 = (bf16[256,256]{1,0:T(8,128)(2,1)S(1)}, bf16[256,256]{1,0:T(8,128)(2,1)S(1)}, u32[]{:S(2)}, u32[]{:S(2)}) collective-permute-start(bf16[256,256]{1,0:T(8,128)(2,1)S(1)} %get-tuple-element.24), channel_id=1, source_target_pairs={{0,0},{1,1},{2,8},{3,9},{4,4},{5,5},{6,12},{7,13},{8,2},{9,3},{10,... | collective-permute-start | bytes 393224 | tf_op jit(solution)/shard_map/ppermute | solution.py:245
  99.2 2.8 %collective-permute-start.29 = (bf16[256,256]{1,0:T(8,128)(2,1)S(1)}, bf16[256,256]{1,0:T(8,128)(2,1)S(1)}, u32[]{:S(2)}, u32[]{:S(2)}) collective-permute-start(bf16[256,256]{1,0:T(8,128)(2,1)S(1)} %get-tuple-element.25), channel_id=1, source_target_pairs={{0,1},{1,0},{2,9},{3,8},{4,5},{5,4},{6,13},{7,12},{8,3},{9,2},{10,... | collective-permute-start | bytes 393224 | tf_op jit(solution)/shard_map/ppermute | solution.py:245
  102.0 1.7 %collective-permute-done.31.refs_3_ = bf16[2,256,256]{2,1,0:T(8,128)(2,1)S(1)} collective-permute-done((bf16[2,256,256]{2,1,0:T(8,128)(2,1)S(1)}, bf16[2,256,256]{2,1,0:T(8,128)(2,1)S(1)}, u32[]{:S(2)}, u32[]{:S(2)}) %collective-permute-start.31) | collective-permute-done | bytes 262176 | tf_op jit(solution)/shard_map/ppermute | solution.py:202
  103.8 1.3 %shard_map.92.part_ref = f32[2,256,256]{2,1,0:T(8,128)S(1)} custom-call(s32[5,8]{1,0:T(8,128)S(1)} %pad_add_fusion.meta, bf16[8,256,256]{2,1,0:T(8,128)(2,1)S(1)} %get-tuple-element.26.own_ref, bf16[8,256,256]{2,1,0:T(8,128)(2,1)S(1)} %collective-permute-done.30.other_ref, bf16[2,256,256]{2,1,0:T(8,128)(2,1)S(1)} %shard_map.90.refs_0_, ...), custom_call_target="tpu_custom_call" | custom-call | flops 536870912 | bytes 6291456 | tf_op jit(solution)/shard_map/pallas_call | solution.py:23
  105.1 2.9 %collective-permute-done.29.other_ref = bf16[256,256]{1,0:T(8,128)(2,1)S(1)} collective-permute-done((bf16[256,256]{1,0:T(8,128)(2,1)S(1)}, bf16[256,256]{1,0:T(8,128)(2,1)S(1)}, u32[]{:S(2)}, u32[]{:S(2)}) %collective-permute-start.29) | collective-permute-done | bytes 131104 | tf_op jit(solution)/shard_map/ppermute | solution.py:245
  108.0 1.6 %shard_map.93 = (f32[2,256,256]{2,1,0:T(8,128)}, bf16[2,256,256]{2,1,0:T(8,128)(2,1)}) custom-call(s32[5,8]{1,0:T(8,128)S(1)} %pad_add_fusion.meta, bf16[256,256]{1,0:T(8,128)(2,1)S(1)} %collective-permute-done.28.same_ref, bf16[256,256]{1,0:T(8,128)(2,1)S(1)} %collective-permute-done.29.other_ref, f32[2,256,256]{2,1,0:T(8,128)S(1)} %shard_map.92.part_ref, ...), custom_call_target="tpu_custom_call" | custom-call | bytes 2097152 | tf_op jit(solution)/shard_map/pallas_call | solution.py:23
  (69 shorter events, 19.9 us)
Async XLA Ops:
  1.1 12.7 %collective-permute-start.5 = (bf16[2,256,256]{2,1,0:T(8,128)(2,1)S(1)}, bf16[2,256,256]{2,1,0:T(8,128)(2,1)S(1)}, u32[]{:S(2)}, u32[]{:S(2)}) collective-permute-start(bf16[2,256,256]{2,1,0:T(8,128)(2,1)S(1)} %bitcast_convert_fusion.refs_0_), channel_id=1, source_target_pairs={{0,2},{1,3},{2,4},{3,5},{4,6},{5,7},{8,10},{9,11},{10,12},{11,13},... | collective-permute-start | bytes 786440 | tf_op jit(solution)/shard_map/ppermute | solution.py:219
  4.3 10.2 %collective-permute-start.6 = (bf16[2,256,256]{2,1,0:T(8,128)(2,1)S(1)}, bf16[2,256,256]{2,1,0:T(8,128)(2,1)S(1)}, u32[]{:S(2)}, u32[]{:S(2)}) collective-permute-start(bf16[2,256,256]{2,1,0:T(8,128)(2,1)S(1)} %bitcast_convert_fusion.refs_0_), channel_id=1, source_target_pairs={{2,0},{3,1},{4,2},{5,3},{6,4},{7,5},{10,8},{11,9},{12,10},{13,11},... | collective-permute-start | bytes 786440 | tf_op jit(solution)/shard_map/ppermute | solution.py:219
  5.6 6.9 %collective-permute-start.1 = (bf16[2,256,256]{2,1,0:T(8,128)(2,1)S(1)}, bf16[2,256,256]{2,1,0:T(8,128)(2,1)S(1)}, u32[]{:S(2)}, u32[]{:S(2)}) collective-permute-start(bf16[2,256,256]{2,1,0:T(8,128)(2,1)S(1)} %bitcast_convert_fusion.refs_0_), channel_id=1, source_target_pairs={{16,0},{24,8},{0,16},{8,24},{17,1},{25,9},{1,17},{9,25},{18,2},{26... | collective-permute-start | bytes 786440 | tf_op jit(solution)/shard_map/ppermute | solution.py:202
  5.9 7.0 %collective-permute-start = (bf16[2,256,256]{2,1,0:T(8,128)(2,1)S(1)}, bf16[2,256,256]{2,1,0:T(8,128)(2,1)S(1)}, u32[]{:S(2)}, u32[]{:S(2)}) collective-permute-start(bf16[2,256,256]{2,1,0:T(8,128)(2,1)S(1)} %bitcast_convert_fusion.refs_0_), channel_id=1, source_target_pairs={{8,0},{0,8},{24,16},{16,24},{9,1},{1,9},{25,17},{17,25},{10,2},{2,... | collective-permute-start | bytes 786440 | tf_op jit(solution)/shard_map/ppermute | solution.py:202
  12.5 8.0 %collective-permute-start.2 = (bf16[1,256,256]{2,1,0:T(8,128)(2,1)S(1)}, bf16[1,256,256]{2,1,0:T(8,128)(2,1)S(1)}, u32[]{:S(2)}, u32[]{:S(2)}) collective-permute-start(bf16[1,256,256]{2,1,0:T(8,128)(2,1)S(1)} %slice.16), channel_id=1, source_target_pairs={{8,0},{0,8},{24,16},{16,24},{9,1},{1,9},{25,17},{17,25},{10,2},{2,... | collective-permute-start | bytes 393224 | tf_op jit(solution)/shard_map/ppermute | solution.py:202
  12.9 7.7 %collective-permute-start.3 = (bf16[1,256,256]{2,1,0:T(8,128)(2,1)S(1)}, bf16[1,256,256]{2,1,0:T(8,128)(2,1)S(1)}, u32[]{:S(2)}, u32[]{:S(2)}) collective-permute-start(bf16[1,256,256]{2,1,0:T(8,128)(2,1)S(1)} %slice.17), channel_id=1, source_target_pairs={{16,0},{24,8},{0,16},{8,24},{17,1},{25,9},{1,17},{9,25},{18,2},{26... | collective-permute-start | bytes 393224 | tf_op jit(solution)/shard_map/ppermute | solution.py:202
  13.8 17.4 %collective-permute-start.7 = (bf16[2,256,256]{2,1,0:T(8,128)(2,1)S(1)}, bf16[2,256,256]{2,1,0:T(8,128)(2,1)S(1)}, u32[]{:S(2)}, u32[]{:S(2)}) collective-permute-start(bf16[2,256,256]{2,1,0:T(8,128)(2,1)S(1)} %collective-permute-done.5.refs_1_), channel_id=1, source_target_pairs={{2,4},{3,5},{4,6},{5,7},{10,12},{11,13},{12,14},{13,15},{18,20},{1... | collective-permute-start | bytes 786440 | tf_op jit(solution)/shard_map/ppermute | solution.py:219
  14.5 16.7 %collective-permute-start.8 = (bf16[2,256,256]{2,1,0:T(8,128)(2,1)S(1)}, bf16[2,256,256]{2,1,0:T(8,128)(2,1)S(1)}, u32[]{:S(2)}, u32[]{:S(2)}) collective-permute-start(bf16[2,256,256]{2,1,0:T(8,128)(2,1)S(1)} %collective-permute-done.6.refs_2_), channel_id=1, source_target_pairs={{2,0},{3,1},{4,2},{5,3},{10,8},{11,9},{12,10},{13,11},{18,16},{19,... | collective-permute-start | bytes 786440 | tf_op jit(solution)/shard_map/ppermute | solution.py:219
  21.3 11.2 %collective-permute-start.10 = (bf16[2,256,256]{2,1,0:T(8,128)(2,1)S(1)}, bf16[2,256,256]{2,1,0:T(8,128)(2,1)S(1)}, u32[]{:S(2)}, u32[]{:S(2)}) collective-permute-start(bf16[2,256,256]{2,1,0:T(8,128)(2,1)S(1)} %shard_map.86.refs_0_), channel_id=1, source_target_pairs={{8,0},{0,8},{24,16},{16,24},{9,1},{1,9},{25,17},{17,25},{10,2},{2,... | collective-permute-start | bytes 786440 | tf_op jit(solution)/shard_map/ppermute | solution.py:202
  22.0 10.6 %collective-permute-start.11 = (bf16[2,256,256]{2,1,0:T(8,128)(2,1)S(1)}, bf16[2,256,256]{2,1,0:T(8,128)(2,1)S(1)}, u32[]{:S(2)}, u32[]{:S(2)}) collective-permute-start(bf16[2,256,256]{2,1,0:T(8,128)(2,1)S(1)} %shard_map.86.refs_0_), channel_id=1, source_target_pairs={{16,0},{24,8},{0,16},{8,24},{17,1},{25,9},{1,17},{9,25},{18,2},{26... | collective-permute-start | bytes 786440 | tf_op jit(solution)/shard_map/ppermute | solution.py:202
  23.2 18.6 %collective-permute-start.4 = (bf16[2,256,256]{2,1,0:T(8,128)(2,1)S(1)}, bf16[2,256,256]{2,1,0:T(8,128)(2,1)S(1)}, u32[]{:S(2)}, u32[]{:S(2)}) collective-permute-start(bf16[2,256,256]{2,1,0:T(8,128)(2,1)S(1)} %shard_map.86.refs_0_), channel_id=1, source_target_pairs={{0,0},{1,1},{2,2},{3,3},{4,16},{5,17},{6,18},{7,19},{8,8},{9,9},{1... | collective-permute-start | bytes 786440 | tf_op jit(solution)/shard_map/ppermute | solution.py:245
  31.2 10.5 %collective-permute-start.9 = (bf16[2,256,256]{2,1,0:T(8,128)(2,1)S(1)}, bf16[2,256,256]{2,1,0:T(8,128)(2,1)S(1)}, u32[]{:S(2)}, u32[]{:S(2)}) collective-permute-start(bf16[2,256,256]{2,1,0:T(8,128)(2,1)S(1)} %broadcast_select_fusion.1), channel_id=1, source_target_pairs={{4,6},{5,7},{2,0},{3,1},{12,14},{13,15},{10,8},{11,9},{20,22},{21,... | collective-permute-start | bytes 786440 | tf_op jit(solution)/shard_map/ppermute | solution.py:219
  42.5 10.3 %collective-permute-start.14 = (bf16[8,256,256]{2,1,0:T(8,128)(2,1)S(1)}, bf16[8,256,256]{2,1,0:T(8,128)(2,1)S(1)}, u32[]{:S(2)}, u32[]{:S(2)}) collective-permute-start(bf16[8,256,256]{2,1,0:T(8,128)(2,1)S(1)} %get-tuple-element.20.own_ref), channel_id=1, source_target_pairs={{1,0},{0,1},{3,2},{2,3},{5,4},{4,5},{7,6},{6,7},{9,8},{8,9},{11,10... | collective-permute-start | bytes 3145736 | tf_op jit(solution)/shard_map/ppermute | solution.py:216
  45.0 7.9 %collective-permute-start.15 = (bf16[2,256,256]{2,1,0:T(8,128)(2,1)S(1)}, bf16[2,256,256]{2,1,0:T(8,128)(2,1)S(1)}, u32[]{:S(2)}, u32[]{:S(2)}) collective-permute-start(bf16[2,256,256]{2,1,0:T(8,128)(2,1)S(1)} %collective-permute-done.10.refs_6_.refs_1_), channel_id=1, source_target_pairs={{16,0},{24,8},{0,16},{8,24},{17,1},{25,9},{1,17},{9,25},{18,2},{26... | collective-permute-start | bytes 786440 | tf_op jit(solution)/shard_map/ppermute | solution.py:202
  45.0 9.3 %collective-permute-start.12 = (bf16[256,256]{1,0:T(8,128)(2,1)S(1)}, bf16[256,256]{1,0:T(8,128)(2,1)S(1)}, u32[]{:S(2)}, u32[]{:S(2)}) collective-permute-start(bf16[256,256]{1,0:T(8,128)(2,1)S(1)} %get-tuple-element.18), channel_id=1, source_target_pairs={{0,0},{1,1},{2,8},{3,9},{4,4},{5,5},{6,12},{7,13},{8,2},{9,3},{10,... | collective-permute-start | bytes 393224 | tf_op jit(solution)/shard_map/ppermute | solution.py:245
  46.9 8.9 %collective-permute-start.13 = (bf16[256,256]{1,0:T(8,128)(2,1)S(1)}, bf16[256,256]{1,0:T(8,128)(2,1)S(1)}, u32[]{:S(2)}, u32[]{:S(2)}) collective-permute-start(bf16[256,256]{1,0:T(8,128)(2,1)S(1)} %get-tuple-element.19), channel_id=1, source_target_pairs={{0,1},{1,0},{2,9},{3,8},{4,5},{5,4},{6,13},{7,12},{8,3},{9,2},{10,... | collective-permute-start | bytes 393224 | tf_op jit(solution)/shard_map/ppermute | solution.py:245
  56.6 7.1 %collective-permute-start.21 = (bf16[2,256,256]{2,1,0:T(8,128)(2,1)S(1)}, bf16[2,256,256]{2,1,0:T(8,128)(2,1)S(1)}, u32[]{:S(2)}, u32[]{:S(2)}) collective-permute-start(bf16[2,256,256]{2,1,0:T(8,128)(2,1)S(1)} %get-tuple-element.23.refs_0_), channel_id=1, source_target_pairs={{0,2},{1,3},{2,4},{3,5},{4,6},{5,7},{8,10},{9,11},{10,12},{11,13},... | collective-permute-start | bytes 786440 | tf_op jit(solution)/shard_map/ppermute | solution.py:219
  57.9 9.7 %collective-permute-start.22 = (bf16[2,256,256]{2,1,0:T(8,128)(2,1)S(1)}, bf16[2,256,256]{2,1,0:T(8,128)(2,1)S(1)}, u32[]{:S(2)}, u32[]{:S(2)}) collective-permute-start(bf16[2,256,256]{2,1,0:T(8,128)(2,1)S(1)} %get-tuple-element.23.refs_0_), channel_id=1, source_target_pairs={{2,0},{3,1},{4,2},{5,3},{6,4},{7,5},{10,8},{11,9},{12,10},{13,11},... | collective-permute-start | bytes 786440 | tf_op jit(solution)/shard_map/ppermute | solution.py:219
  59.2 9.7 %collective-permute-start.17 = (bf16[2,256,256]{2,1,0:T(8,128)(2,1)S(1)}, bf16[2,256,256]{2,1,0:T(8,128)(2,1)S(1)}, u32[]{:S(2)}, u32[]{:S(2)}) collective-permute-start(bf16[2,256,256]{2,1,0:T(8,128)(2,1)S(1)} %get-tuple-element.23.refs_0_), channel_id=1, source_target_pairs={{16,0},{24,8},{0,16},{8,24},{17,1},{25,9},{1,17},{9,25},{18,2},{26... | collective-permute-start | bytes 786440 | tf_op jit(solution)/shard_map/ppermute | solution.py:202
  60.7 8.6 %collective-permute-start.16 = (bf16[2,256,256]{2,1,0:T(8,128)(2,1)S(1)}, bf16[2,256,256]{2,1,0:T(8,128)(2,1)S(1)}, u32[]{:S(2)}, u32[]{:S(2)}) collective-permute-start(bf16[2,256,256]{2,1,0:T(8,128)(2,1)S(1)} %get-tuple-element.23.refs_0_), channel_id=1, source_target_pairs={{8,0},{0,8},{24,16},{16,24},{9,1},{1,9},{25,17},{17,25},{10,2},{2,... | collective-permute-start | bytes 786440 | tf_op jit(solution)/shard_map/ppermute | solution.py:202
  63.7 16.7 %collective-permute-start.23 = (bf16[2,256,256]{2,1,0:T(8,128)(2,1)S(1)}, bf16[2,256,256]{2,1,0:T(8,128)(2,1)S(1)}, u32[]{:S(2)}, u32[]{:S(2)}) collective-permute-start(bf16[2,256,256]{2,1,0:T(8,128)(2,1)S(1)} %collective-permute-done.21.refs_1_), channel_id=1, source_target_pairs={{2,4},{3,5},{4,6},{5,7},{10,12},{11,13},{12,14},{13,15},{18,20},{1... | collective-permute-start | bytes 786440 | tf_op jit(solution)/shard_map/ppermute | solution.py:219
  67.6 12.8 %collective-permute-start.24 = (bf16[2,256,256]{2,1,0:T(8,128)(2,1)S(1)}, bf16[2,256,256]{2,1,0:T(8,128)(2,1)S(1)}, u32[]{:S(2)}, u32[]{:S(2)}) collective-permute-start(bf16[2,256,256]{2,1,0:T(8,128)(2,1)S(1)} %collective-permute-done.22.refs_2_), channel_id=1, source_target_pairs={{2,0},{3,1},{4,2},{5,3},{10,8},{11,9},{12,10},{13,11},{18,16},{19,... | collective-permute-start | bytes 786440 | tf_op jit(solution)/shard_map/ppermute | solution.py:219
  68.9 3.9 %collective-permute-start.18 = (bf16[1,256,256]{2,1,0:T(8,128)(2,1)S(1)}, bf16[1,256,256]{2,1,0:T(8,128)(2,1)S(1)}, u32[]{:S(2)}, u32[]{:S(2)}) collective-permute-start(bf16[1,256,256]{2,1,0:T(8,128)(2,1)S(1)} %slice.18), channel_id=1, source_target_pairs={{8,0},{0,8},{24,16},{16,24},{9,1},{1,9},{25,17},{17,25},{10,2},{2,... | collective-permute-start | bytes 393224 | tf_op jit(solution)/shard_map/ppermute | solution.py:202
  69.3 4.5 %collective-permute-start.19 = (bf16[1,256,256]{2,1,0:T(8,128)(2,1)S(1)}, bf16[1,256,256]{2,1,0:T(8,128)(2,1)S(1)}, u32[]{:S(2)}, u32[]{:S(2)}) collective-permute-start(bf16[1,256,256]{2,1,0:T(8,128)(2,1)S(1)} %slice.19), channel_id=1, source_target_pairs={{16,0},{24,8},{0,16},{8,24},{17,1},{25,9},{1,17},{9,25},{18,2},{26... | collective-permute-start | bytes 393224 | tf_op jit(solution)/shard_map/ppermute | solution.py:202
  74.5 16.2 %collective-permute-start.20 = (bf16[2,256,256]{2,1,0:T(8,128)(2,1)S(1)}, bf16[2,256,256]{2,1,0:T(8,128)(2,1)S(1)}, u32[]{:S(2)}, u32[]{:S(2)}) collective-permute-start(bf16[2,256,256]{2,1,0:T(8,128)(2,1)S(1)} %shard_map.90.refs_0_), channel_id=1, source_target_pairs={{0,0},{1,1},{2,2},{3,3},{4,16},{5,17},{6,18},{7,19},{8,8},{9,9},{1... | collective-permute-start | bytes 786440 | tf_op jit(solution)/shard_map/ppermute | solution.py:245
  80.1 10.6 %collective-permute-start.26 = (bf16[2,256,256]{2,1,0:T(8,128)(2,1)S(1)}, bf16[2,256,256]{2,1,0:T(8,128)(2,1)S(1)}, u32[]{:S(2)}, u32[]{:S(2)}) collective-permute-start(bf16[2,256,256]{2,1,0:T(8,128)(2,1)S(1)} %shard_map.90.refs_0_), channel_id=1, source_target_pairs={{8,0},{0,8},{24,16},{16,24},{9,1},{1,9},{25,17},{17,25},{10,2},{2,... | collective-permute-start | bytes 786440 | tf_op jit(solution)/shard_map/ppermute | solution.py:202
  80.4 10.3 %collective-permute-start.27 = (bf16[2,256,256]{2,1,0:T(8,128)(2,1)S(1)}, bf16[2,256,256]{2,1,0:T(8,128)(2,1)S(1)}, u32[]{:S(2)}, u32[]{:S(2)}) collective-permute-start(bf16[2,256,256]{2,1,0:T(8,128)(2,1)S(1)} %shard_map.90.refs_0_), channel_id=1, source_target_pairs={{16,0},{24,8},{0,16},{8,24},{17,1},{25,9},{1,17},{9,25},{18,2},{26... | collective-permute-start | bytes 786440 | tf_op jit(solution)/shard_map/ppermute | solution.py:202
  80.4 10.3 %collective-permute-start.25 = (bf16[2,256,256]{2,1,0:T(8,128)(2,1)S(1)}, bf16[2,256,256]{2,1,0:T(8,128)(2,1)S(1)}, u32[]{:S(2)}, u32[]{:S(2)}) collective-permute-start(bf16[2,256,256]{2,1,0:T(8,128)(2,1)S(1)} %broadcast_select_fusion), channel_id=1, source_target_pairs={{4,6},{5,7},{2,0},{3,1},{12,14},{13,15},{10,8},{11,9},{20,22},{21,... | collective-permute-start | bytes 786440 | tf_op jit(solution)/shard_map/ppermute | solution.py:219
  91.5 12.3 %collective-permute-start.30 = (bf16[8,256,256]{2,1,0:T(8,128)(2,1)S(1)}, bf16[8,256,256]{2,1,0:T(8,128)(2,1)S(1)}, u32[]{:S(2)}, u32[]{:S(2)}) collective-permute-start(bf16[8,256,256]{2,1,0:T(8,128)(2,1)S(1)} %get-tuple-element.26.own_ref), channel_id=1, source_target_pairs={{1,0},{0,1},{3,2},{2,3},{5,4},{4,5},{7,6},{6,7},{9,8},{8,9},{11,10... | collective-permute-start | bytes 3145736 | tf_op jit(solution)/shard_map/ppermute | solution.py:216
  94.7 9.1 %collective-permute-start.31 = (bf16[2,256,256]{2,1,0:T(8,128)(2,1)S(1)}, bf16[2,256,256]{2,1,0:T(8,128)(2,1)S(1)}, u32[]{:S(2)}, u32[]{:S(2)}) collective-permute-start(bf16[2,256,256]{2,1,0:T(8,128)(2,1)S(1)} %collective-permute-done.26.refs_6_.refs_1_), channel_id=1, source_target_pairs={{16,0},{24,8},{0,16},{8,24},{17,1},{25,9},{1,17},{9,25},{18,2},{26... | collective-permute-start | bytes 786440 | tf_op jit(solution)/shard_map/ppermute | solution.py:202
  97.2 7.9 %collective-permute-start.28 = (bf16[256,256]{1,0:T(8,128)(2,1)S(1)}, bf16[256,256]{1,0:T(8,128)(2,1)S(1)}, u32[]{:S(2)}, u32[]{:S(2)}) collective-permute-start(bf16[256,256]{1,0:T(8,128)(2,1)S(1)} %get-tuple-element.24), channel_id=1, source_target_pairs={{0,0},{1,1},{2,8},{3,9},{4,4},{5,5},{6,12},{7,13},{8,2},{9,3},{10,... | collective-permute-start | bytes 393224 | tf_op jit(solution)/shard_map/ppermute | solution.py:245
  99.2 8.8 %collective-permute-start.29 = (bf16[256,256]{1,0:T(8,128)(2,1)S(1)}, bf16[256,256]{1,0:T(8,128)(2,1)S(1)}, u32[]{:S(2)}, u32[]{:S(2)}) collective-permute-start(bf16[256,256]{1,0:T(8,128)(2,1)S(1)} %get-tuple-element.25), channel_id=1, source_target_pairs={{0,1},{1,0},{2,9},{3,8},{4,5},{5,4},{6,13},{7,12},{8,3},{9,2},{10,... | collective-permute-start | bytes 393224 | tf_op jit(solution)/shard_map/ppermute | solution.py:245
  (5 other events, 42.3 us)
where the time goes:
time: 111 us; the launch traced here: 110 us
  starting transfers between devices  53.7 us (48%)
  waiting for transfers between devices  39.1 us (35%)
  Pallas kernels  9.02 us (8%)
  local copies, waits for them, and re-layouts  4.64 us (4%)
  other arithmetic  2.83 us (3%)
    ppermute x6, starting transfers between devices, crossing(): return lax.ppermute(x, ('row', 'col'), pairs)  22.9 us
    ppermute x6, waiting for transfers between devices, crossing(): return lax.ppermute(x, ('row', 'col'), pairs)  22.6 us
    ppermute x10, starting transfers between devices, along(): lax.ppermute(x, 'col', [(2 * at + k, 2 * (at + hop) + k) for at, hop in h...  13.6 us
    ppermute x14, waiting for transfers between devices, from_row(): return lax.ppermute(x, 'row', [(r ^ step, r) for r in range(rows)])  11.5 us
    ppermute x14, starting transfers between devices, from_row(): return lax.ppermute(x, 'row', [(r ^ step, r) for r in range(rows)])  11.5 us
    pallas_call x9, Pallas kernels, call(): pl.pallas_call(body, out_shape=out_shape, in_specs=in_specs, out_specs=VM...  9.02 us
    ppermute x2, starting transfers between devices, swapped(): return lax.ppermute(x, 'col', [(c ^ 1, c) for c in range(cols)])  5.61 us
    ppermute x10, waiting for transfers between devices, along(): lax.ppermute(x, 'col', [(2 * at + k, 2 * (at + hop) + k) for at, hop in h...  4.96 us
  transfers between devices with their start and end apart: 32, of which 11 were waited for; matrix products, arithmetic and copies ran while one was open for 3% of the time, Pallas kernels for 5%

commit v1 on v0

--- a/solution.py
+++ b/solution.py
@@ -94,34 +94,32 @@
     return call(body, shape, [VMEM] * (1 + len(pieces)), flops, moved, kept, *pieces)
 
 
-def placed(meta, ref, hops, out_ref):
-    orb_rows = ref.shape[0]
-    halves = out_ref.shape[0] // orb_rows
-    for hop in hops:
-        spot = meta[2 * orb_rows, 1] // 2 + hop
-
-        @pl.when(jnp.logical_and(spot >= 0, spot < halves))
-        def _():
-            out_ref[pl.ds(spot * orb_rows, orb_rows)] = ref[...]
-
-
-def column_body(places, meta, crossing_ref, *refs):
-    out_ref, same_ref, other_ref = refs[-3:]
+def parted_body(meta, crossing_ref, *refs):
+    same_ref, other_ref = refs[-2:]
     side = meta[2 * crossing_ref.shape[0], 1] % 2
-    for ref, hops in zip(refs, places):
-        placed(meta, ref, hops, out_ref)
     same_ref[...] = crossing_ref[side]
     other_ref[...] = crossing_ref[1 - side]
 
 
-def whole_column(meta, halves, pieces, places, crossing, others):
-    orb_rows, virt, _ = pieces[0].shape
-    block = jax.ShapeDtypeStruct((virt, virt), jnp.bfloat16)
-    shape = (jax.ShapeDtypeStruct((orb_rows * halves, virt, virt), jnp.bfloat16), block, block)
-    operands = [crossing, *pieces, *others]
-    moved = 4 * orb_rows * (halves + 1) * virt**2
-    body = functools.partial(column_body, places)
-    return call(body, shape, [SMEM] + [VMEM] * len(operands), 0, moved, meta, *operands)
+def parted(meta, crossing, others):
+    block = jax.ShapeDtypeStruct(crossing.shape[1:], crossing.dtype)
+    in_specs = [SMEM] + [VMEM] * (1 + len(others))
+    return call(parted_body, (block, block), in_specs, 0, 4 * crossing.size, meta, crossing, *others)
+
+
+def tied_body(*refs):
+    pass
+
+
+def tied(x, *others):
+    return pl.pallas_call(
+        tied_body,
+        out_shape=jax.ShapeDtypeStruct(x.shape, x.dtype),
+        in_specs=[VMEM] * (1 + len(others)),
+        out_specs=VMEM,
+        input_output_aliases={0: 0},
+        compiler_params=pltpu.CompilerParams(vmem_limit_bytes=VMEM_BYTES),
+    )(x, *others)
 
 
 def masked_pair(meta, orbital, blocks):
@@ -215,26 +213,7 @@
     def swapped(x):
         return lax.ppermute(x, "col", [(c ^ 1, c) for c in range(cols)])
 
-    def along(x, hops):
-        return lax.ppermute(
-            x, "col", [(2 * at + k, 2 * (at + hop) + k) for at, hop in hops for k in range(2)]
-        )
-
-    def relayed(x):
-        pieces, places = [x], [(0,)]
-        up = down = x
-        for stage in range(1, halves):
-            ups = [(at, 1) for at in range(stage - 1, halves - 1)]
-            downs = [(at, -1) for at in range(1, halves - stage + 1)]
-            if stage - 1 > halves - stage:
-                up = down = along(jnp.where(my_col // 2 >= stage - 1, up, down), ups + downs)
-                pieces.append(up)
-                places.append((-stage, stage))
-            else:
-                up, down = along(up, ups), along(down, downs)
-                pieces += [up, down]
-                places += [(-stage,), (stage,)]
-        return pieces, tuple(places)
+    one_core = [[2 * at + side for at in range(halves)] for side in range(2)]
 
     def crossing(x, place, flip=0):
         pairs = []
@@ -272,11 +251,12 @@
 
     for sweep_index in range(ITERS):
         a_pieces = row_gathered(half, True)
-        column, places = relayed(half)
+        own = lax.all_gather(half, "col", axis=0, tiled=True, axis_index_groups=one_core)
         coupled = coupled_blocks(rows, kept, a_pieces)
         c_pieces = row_gathered(coupled, False)
         half_way = crossing(coupled, high_parts)
-        own, same, other = whole_column(meta, halves, column, places, half_way, c_pieces[1:3])
+        same, other = parted(meta, half_way, c_pieces[1:3])
+        own = tied(own, same)
         same, other = crossing(same, last_bits), crossing(other, last_bits, 1)
         part = first_update(rows, meta, own, swapped(own), c_pieces, state, coulomb_own, inverse)
         state, half = second_update(meta, same, other, part, inverse)

time: 111 us -> 131 us (1.18)
  starting transfers between devices: 53.7 us -> 23.8 us
  waiting for transfers between devices: 39.1 us -> 59.4 us
  between operations: 0.4 us -> 13.7 us
  local copies, waits for them, and re-layouts: 4.64 us -> 16.8 us
  Pallas kernels: 9.02 us -> 11.4 us
    ppermute x10 -> x0, starting transfers between devices: 13.6 us -> none  [along(): lax.ppermute(x, 'col', [(2 * at + k, 2 * (at + hop) + k) for at, hop in h...]
    ppermute x6, waiting for transfers between devices: 22.6 us -> 36.1 us  [crossing(): return lax.ppermute(x, ('row', 'col'), pairs)]
    ppermute x14, waiting for transfers between devices: 11.5 us -> 23.2 us  [from_row(): return lax.ppermute(x, 'row', [(r ^ step, r) for r in range(rows)])]
    unnamed x10 -> x52, local copies, waits for them, and re-layouts: 2.93 us -> 13.7 us
    ppermute x6, starting transfers between devices: 22.9 us -> 15.3 us  [crossing(): return lax.ppermute(x, ('row', 'col'), pairs)]
    ppermute x10 -> x0, waiting for transfers between devices: 4.96 us -> none  [along(): lax.ppermute(x, 'col', [(2 * at + k, 2 * (at + hop) + k) for at, hop in h...]
    ppermute x14, starting transfers between devices: 11.5 us -> 6.86 us  [from_row(): return lax.ppermute(x, 'row', [(r ^ step, r) for r in range(rows)])]
    ppermute x2, starting transfers between devices: 5.61 us -> 1.6 us  [swapped(): return lax.ppermute(x, 'col', [(c ^ 1, c) for c in range(cols)])]
  transfers between devices with their start and end apart: 32 -> 24, of which waited for: 11 -> 10; matrix products, arithmetic and copies ran while one was open for 3% -> 4% of each run, Pallas kernels for 5% -> 6%
where the time goes in v1:
time: 131 us; the launch traced here: 129 us
  waiting for transfers between devices  59.4 us (45%)
  starting transfers between devices  23.8 us (18%)
  local copies, waits for them, and re-layouts  16.8 us (13%)
  between operations  13.7 us (10%)
  Pallas kernels  11.4 us (9%)
  other arithmetic  3.46 us (3%)
    ppermute x6, waiting for transfers between devices, crossing(): return lax.ppermute(x, ('row', 'col'), pairs)  36.1 us
    ppermute x14, waiting for transfers between devices, from_row(): return lax.ppermute(x, 'row', [(r ^ step, r) for r in range(rows)])  23.2 us
    ppermute x6, starting transfers between devices, crossing(): return lax.ppermute(x, ('row', 'col'), pairs)  15.3 us
    unnamed x52, local copies, waits for them, and re-layouts  13.7 us
    pallas_call x9, Pallas kernels, call(): pl.pallas_call(body, out_shape=out_shape, in_specs=in_specs, out_specs=VM...  11.4 us
    ppermute x14, starting transfers between devices, from_row(): return lax.ppermute(x, 'row', [(r ^ step, r) for r in range(rows)])  6.86 us
  transfers between devices with their start and end apart: 24, of which 10 were waited for; matrix products, arithmetic and copies ran while one was open for 4% of the time, Pallas kernels for 6%

profile of v1, /device:TPU:7, one launch (start us, length us, event | category | flops | bytes accessed | tf_op | source)
XLA Modules:
  0.0 128.5 jit_solution(17905197665481877228)
XLA Ops:
  6.5 1.8 %bitcast_convert_fusion.refs_0_ = bf16[2,256,256]{2,1,0:T(8,128)(2,1)} fusion(f32[2,1,256,256]{3,2,1,0:T(8,128)} %param.8), kind=kLoop, calls=%fused_computation.12 | loop fusion | flops 131072 | bytes 786432 | tf_op jit(solution)/shard_map/convert_element_type | solution.py:233
  8.8 0.9 dynamic-slice_reduce_fusion
  11.3 4.5 %collective-permute-done.1.refs_2_ = bf16[2,256,256]{2,1,0:T(8,128)(2,1)S(1)} collective-permute-done((bf16[2,256,256]{2,1,0:T(8,128)(2,1)}, bf16[2,256,256]{2,1,0:T(8,128)(2,1)S(1)}, u32[]{:S(2)}, u32[]{:S(2)}) %collective-permute-start.1) | collective-permute-done | bytes 262176 | tf_op jit(solution)/shard_map/ppermute | solution.py:200
  18.7 1.6 %copy-done.6 = bf16[2,8,256,256]{3,2,1,0:T(8,128)(2,1)S(1)} copy-done((bf16[2,8,256,256]{3,2,1,0:T(8,128)(2,1)S(1)}, bf16[2,8,256,256]{3,2,1,0:T(8,128)(2,1)}, u32[]{:S(2)}) %copy-start.6) | copy-done | bytes 2097176
  21.6 0.9 shard_map.85
  22.6 1.7 %shard_map.86.refs_0_ = bf16[2,256,256]{2,1,0:T(8,128)(2,1)S(1)} custom-call(bf16[4,512,512]{2,1,0:T(8,128)(2,1)S(1)} %get-tuple-element.15.k_ref, bf16[2,256,256]{2,1,0:T(8,128)(2,1)S(1)} %copy-done.5, bf16[2,256,256]{2,1,0:T(8,128)(2,1)S(1)} %copy-done.17, bf16[2,256,256]{2,1,0:T(8,128)(2,1)S(1)} %collective-permute-done.1.refs_2_, ...), custom_call_target="tpu_custom_call" | custom-call | flops 536870912 | bytes 3145728 | tf_op jit(solution)/shard_map/pallas_call | solution.py:23
  24.3 1.2 collective-permute-start.6
  25.5 1.2 collective-permute-start.5
  26.7 4.2 %collective-permute-start.4 = (bf16[2,256,256]{2,1,0:T(8,128)(2,1)S(1)}, bf16[2,256,256]{2,1,0:T(8,128)(2,1)S(1)}, u32[]{:S(2)}, u32[]{:S(2)}) collective-permute-start(bf16[2,256,256]{2,1,0:T(8,128)(2,1)S(1)} %shard_map.86.refs_0_), channel_id=1, source_target_pairs={{0,0},{1,1},{2,2},{3,3},{4,16},{5,17},{6,18},{7,19},{8,8},{9,9},{1... | collective-permute-start | bytes 786440 | tf_op jit(solution)/shard_map/ppermute | solution.py:224
  31.6 17.8 %collective-permute-done.4.crossing_ref = bf16[2,256,256]{2,1,0:T(8,128)(2,1)S(1)} collective-permute-done((bf16[2,256,256]{2,1,0:T(8,128)(2,1)S(1)}, bf16[2,256,256]{2,1,0:T(8,128)(2,1)S(1)}, u32[]{:S(2)}, u32[]{:S(2)}) %collective-permute-start.4) | collective-permute-done | bytes 262176 | tf_op jit(solution)/shard_map/ppermute | solution.py:224
  52.1 1.2 copy-done.1
  53.4 0.9 collective-permute-start.9
  54.2 1.0 copy-done.2
  55.3 4.1 %collective-permute-start.7 = (bf16[256,256]{1,0:T(8,128)(2,1)S(1)}, bf16[256,256]{1,0:T(8,128)(2,1)S(1)}, u32[]{:S(2)}, u32[]{:S(2)}) collective-permute-start(bf16[256,256]{1,0:T(8,128)(2,1)S(1)} %get-tuple-element.16.refs_1_), channel_id=1, source_target_pairs={{0,0},{1,1},{2,8},{3,9},{4,4},{5,5},{6,12},{7,13},{8,2},{9,3},{10,... | collective-permute-start | bytes 393224 | tf_op jit(solution)/shard_map/ppermute | solution.py:224
  59.5 3.7 %collective-permute-done.10.refs_3_ = bf16[2,256,256]{2,1,0:T(8,128)(2,1)S(1)} collective-permute-done((bf16[2,256,256]{2,1,0:T(8,128)(2,1)S(1)}, bf16[2,256,256]{2,1,0:T(8,128)(2,1)S(1)}, u32[]{:S(2)}, u32[]{:S(2)}) %collective-permute-start.10) | collective-permute-done | bytes 262176 | tf_op jit(solution)/shard_map/ppermute | solution.py:200
  63.2 1.2 copy-done.3
  64.4 1.3 %shard_map.89.part_ref = f32[2,256,256]{2,1,0:T(8,128)S(1)} custom-call(s32[5,8]{1,0:T(8,128)S(1)} %pad_add_fusion.meta, bf16[8,256,256]{2,1,0:T(8,128)(2,1)S(1)} %copy-done.3, bf16[8,256,256]{2,1,0:T(8,128)(2,1)S(1)} %collective-permute-done.9.other_ref, bf16[2,256,256]{2,1,0:T(8,128)(2,1)S(1)} %copy-done.15, bf16[2,256,256]{2,1,0:T(8,128)(2,1)S(1)} %copy-done.11, ...), custom_call_target="tpu_custom_call" | custom-call | flops 536870912 | bytes 6291456 | tf_op jit(solution)/shard_map/pallas_call | solution.py:23
  65.8 1.5 %shard_map.90 = (f32[2,256,256]{2,1,0:T(8,128)S(1)}, bf16[2,256,256]{2,1,0:T(8,128)(2,1)}) custom-call(s32[5,8]{1,0:T(8,128)S(1)} %pad_add_fusion.meta, bf16[256,256]{1,0:T(8,128)(2,1)S(1)} %collective-permute-done.7.same_ref, bf16[256,256]{1,0:T(8,128)(2,1)S(1)} %collective-permute-done.8.other_ref, f32[2,256,256]{2,1,0:T(8,128)S(1)} %shard_map.89.part_ref, ...), custom_call_target="tpu_custom_call" | custom-call | bytes 2097152 | tf_op jit(solution)/shard_map/pallas_call | solution.py:23
  68.6 6.8 %collective-permute-done.12.refs_2_ = bf16[2,256,256]{2,1,0:T(8,128)(2,1)S(1)} collective-permute-done((bf16[2,256,256]{2,1,0:T(8,128)(2,1)}, bf16[2,256,256]{2,1,0:T(8,128)(2,1)S(1)}, u32[]{:S(2)}, u32[]{:S(2)}) %collective-permute-start.12) | collective-permute-done | bytes 262176 | tf_op jit(solution)/shard_map/ppermute | solution.py:200
  75.8 0.9 collective-permute-start.14
  76.7 3.0 %collective-permute-done.13.refs_3_ = bf16[1,256,256]{2,1,0:T(8,128)(2,1)S(1)} collective-permute-done((bf16[1,256,256]{2,1,0:T(8,128)(2,1)S(1)}, bf16[1,256,256]{2,1,0:T(8,128)(2,1)S(1)}, u32[]{:S(2)}, u32[]{:S(2)}) %collective-permute-start.13) | collective-permute-done | bytes 131104 | tf_op jit(solution)/shard_map/ppermute | solution.py:200
  80.1 1.7 %shard_map.91.refs_0_ = bf16[2,256,256]{2,1,0:T(8,128)(2,1)S(1)} custom-call(bf16[4,512,512]{2,1,0:T(8,128)(2,1)S(1)} %get-tuple-element.15.k_ref, bf16[2,256,256]{2,1,0:T(8,128)(2,1)} %get-tuple-element.20.refs_0_, bf16[2,256,256]{2,1,0:T(8,128)(2,1)S(1)} %collective-permute-done.11.refs_1_, bf16[2,256,256]{2,1,0:T(8,128)(2,1)S(1)} %collective-permute-done.12.refs_2_, ...), custom_call_target="tpu_custom_call" | custom-call | flops 536870912 | bytes 3145728 | tf_op jit(solution)/shard_map/pallas_call | solution.py:23
  81.7 0.9 collective-permute-start.17
  83.4 2.1 %collective-permute-start.15 = (bf16[2,256,256]{2,1,0:T(8,128)(2,1)S(1)}, bf16[2,256,256]{2,1,0:T(8,128)(2,1)S(1)}, u32[]{:S(2)}, u32[]{:S(2)}) collective-permute-start(bf16[2,256,256]{2,1,0:T(8,128)(2,1)S(1)} %shard_map.91.refs_0_), channel_id=1, source_target_pairs={{0,0},{1,1},{2,2},{3,3},{4,16},{5,17},{6,18},{7,19},{8,8},{9,9},{1... | collective-permute-start | bytes 786440 | tf_op jit(solution)/shard_map/ppermute | solution.py:224
  86.2 1.2 collective-permute-done.17.refs_1_.refs_2_
  88.2 18.3 %collective-permute-done.15.crossing_ref = bf16[2,256,256]{2,1,0:T(8,128)(2,1)S(1)} collective-permute-done((bf16[2,256,256]{2,1,0:T(8,128)(2,1)S(1)}, bf16[2,256,256]{2,1,0:T(8,128)(2,1)S(1)}, u32[]{:S(2)}, u32[]{:S(2)}) %collective-permute-start.15) | collective-permute-done | bytes 262176 | tf_op jit(solution)/shard_map/ppermute | solution.py:224
  107.8 1.2 copy-done.4
  109.9 4.9 %collective-permute-start.18 = (bf16[256,256]{1,0:T(8,128)(2,1)S(1)}, bf16[256,256]{1,0:T(8,128)(2,1)S(1)}, u32[]{:S(2)}, u32[]{:S(2)}) collective-permute-start(bf16[256,256]{1,0:T(8,128)(2,1)S(1)} %get-tuple-element.21.refs_1_), channel_id=1, source_target_pairs={{0,0},{1,1},{2,8},{3,9},{4,4},{5,5},{6,12},{7,13},{8,2},{9,3},{10,... | collective-permute-start | bytes 393224 | tf_op jit(solution)/shard_map/ppermute | solution.py:224
  114.8 2.8 %collective-permute-done.21.refs_3_ = bf16[2,256,256]{2,1,0:T(8,128)(2,1)S(1)} collective-permute-done((bf16[2,256,256]{2,1,0:T(8,128)(2,1)S(1)}, bf16[2,256,256]{2,1,0:T(8,128)(2,1)S(1)}, u32[]{:S(2)}, u32[]{:S(2)}) %collective-permute-start.21) | collective-permute-done | bytes 262176 | tf_op jit(solution)/shard_map/ppermute | solution.py:200
  117.6 1.0 copy-done.19
  118.7 1.4 %shard_map.94.part_ref = f32[2,256,256]{2,1,0:T(8,128)S(1)} custom-call(s32[5,8]{1,0:T(8,128)S(1)} %pad_add_fusion.meta, bf16[8,256,256]{2,1,0:T(8,128)(2,1)S(1)} %shard_map.93.own_ref, bf16[8,256,256]{2,1,0:T(8,128)(2,1)S(1)} %collective-permute-done.20.other_ref, bf16[2,256,256]{2,1,0:T(8,128)(2,1)S(1)} %copy-done.13, ...), custom_call_target="tpu_custom_call" | custom-call | flops 536870912 | bytes 6291456 | tf_op jit(solution)/shard_map/pallas_call | solution.py:23
  120.1 1.6 %shard_map.95 = (f32[2,256,256]{2,1,0:T(8,128)}, bf16[2,256,256]{2,1,0:T(8,128)(2,1)}) custom-call(s32[5,8]{1,0:T(8,128)S(1)} %pad_add_fusion.meta, bf16[256,256]{1,0:T(8,128)(2,1)S(1)} %collective-permute-done.18.same_ref, bf16[256,256]{1,0:T(8,128)(2,1)S(1)} %collective-permute-done.19.other_ref, f32[2,256,256]{2,1,0:T(8,128)S(1)} %shard_map.94.part_ref, ...), custom_call_target="tpu_custom_call" | custom-call | bytes 2097152 | tf_op jit(solution)/shard_map/pallas_call | solution.py:23
  (97 shorter events, 16.4 us)
Async XLA Ops:
  6.5 3.9 %copy-start = (s32[2,8,8]{2,1,0:T(8,128)S(1)}, s32[2,8,8]{2,1,0:T(8,128)}, u32[]{:S(2)}) copy-start(s32[2,8,8]{2,1,0:T(8,128)} %param.12) | copy-start | bytes 1540
  6.5 45.6 %all-gather.3.cloned.1.call-start = ((), (), s32[]{:S(2)}) async-start(), calls=%async_computation | async-start | bytes 1310720 | tf_op jit(solution)/shard_map/all_gather | solution.py:254
  8.3 14.3 %copy-start.5 = (bf16[2,256,256]{2,1,0:T(8,128)(2,1)S(1)}, bf16[2,256,256]{2,1,0:T(8,128)(2,1)}, u32[]{:S(2)}) copy-start(bf16[2,256,256]{2,1,0:T(8,128)(2,1)} %bitcast_convert_fusion.refs_0_) | copy-start | bytes 786436
  8.3 99.5 %all-gather.5.cloned.1.call-start = ((), (), s32[]{:S(2)}) async-start(), calls=%async_computation.1 | async-start | bytes 1310720 | tf_op jit(solution)/shard_map/all_gather | solution.py:254
  8.4 7.5 %collective-permute-start.1 = (bf16[2,256,256]{2,1,0:T(8,128)(2,1)}, bf16[2,256,256]{2,1,0:T(8,128)(2,1)S(1)}, u32[]{:S(2)}, u32[]{:S(2)}) collective-permute-start(bf16[2,256,256]{2,1,0:T(8,128)(2,1)} %bitcast_convert_fusion.refs_0_), channel_id=1, source_target_pairs={{16,0},{24,8},{0,16},{8,24},{17,1},{25,9},{1,17},{9,25},{18,2},{26... | collective-permute-start | bytes 786440 | tf_op jit(solution)/shard_map/ppermute | solution.py:200
  8.7 8.1 %collective-permute-start = (bf16[2,256,256]{2,1,0:T(8,128)(2,1)}, bf16[2,256,256]{2,1,0:T(8,128)(2,1)S(1)}, u32[]{:S(2)}, u32[]{:S(2)}) collective-permute-start(bf16[2,256,256]{2,1,0:T(8,128)(2,1)} %bitcast_convert_fusion.refs_0_), channel_id=1, source_target_pairs={{8,0},{0,8},{24,16},{16,24},{9,1},{1,9},{25,17},{17,25},{10,2},{2,... | collective-permute-start | bytes 786440 | tf_op jit(solution)/shard_map/ppermute | solution.py:200
  16.5 6.1 %collective-permute-start.2 = (bf16[1,256,256]{2,1,0:T(8,128)(2,1)}, bf16[1,256,256]{2,1,0:T(8,128)(2,1)}, u32[]{:S(2)}, u32[]{:S(2)}) collective-permute-start(bf16[1,256,256]{2,1,0:T(8,128)(2,1)} %slice.16), channel_id=1, source_target_pairs={{8,0},{0,8},{24,16},{16,24},{9,1},{1,9},{25,17},{17,25},{10,2},{2,... | collective-permute-start | bytes 393224 | tf_op jit(solution)/shard_map/ppermute | solution.py:200
  16.8 1.9 %copy-start.16 = (bf16[2,256,256]{2,1,0:T(8,128)(2,1)}, bf16[2,256,256]{2,1,0:T(8,128)(2,1)S(1)}, u32[]{:S(2)}) copy-start(bf16[2,256,256]{2,1,0:T(8,128)(2,1)S(1)} %collective-permute-done.refs_1_) | copy-start | bytes 786436
  17.5 5.1 %collective-permute-start.3 = (bf16[1,256,256]{2,1,0:T(8,128)(2,1)}, bf16[1,256,256]{2,1,0:T(8,128)(2,1)}, u32[]{:S(2)}, u32[]{:S(2)}) collective-permute-start(bf16[1,256,256]{2,1,0:T(8,128)(2,1)} %slice.17), channel_id=1, source_target_pairs={{16,0},{24,8},{0,16},{8,24},{17,1},{25,9},{1,17},{9,25},{18,2},{26... | collective-permute-start | bytes 393224 | tf_op jit(solution)/shard_map/ppermute | solution.py:200
  24.3 38.9 %copy-start.7 = (f32[2,1,256,256]{3,2,1,0:T(8,128)S(1)}, f32[2,1,256,256]{3,2,1,0:T(8,128)}, u32[]{:S(2)}) copy-start(f32[2,1,256,256]{3,2,1,0:T(8,128)} %param.8) | copy-start | bytes 1572868
  24.3 7.3 %collective-permute-start.6 = (bf16[2,256,256]{2,1,0:T(8,128)(2,1)S(1)}, bf16[2,256,256]{2,1,0:T(8,128)(2,1)S(1)}, u32[]{:S(2)}, u32[]{:S(2)}) collective-permute-start(bf16[2,256,256]{2,1,0:T(8,128)(2,1)S(1)} %shard_map.86.refs_0_), channel_id=1, source_target_pairs={{16,0},{24,8},{0,16},{8,24},{17,1},{25,9},{1,17},{9,25},{18,2},{26... | collective-permute-start | bytes 786440 | tf_op jit(solution)/shard_map/ppermute | solution.py:200
  25.5 6.1 %collective-permute-start.5 = (bf16[2,256,256]{2,1,0:T(8,128)(2,1)S(1)}, bf16[2,256,256]{2,1,0:T(8,128)(2,1)S(1)}, u32[]{:S(2)}, u32[]{:S(2)}) collective-permute-start(bf16[2,256,256]{2,1,0:T(8,128)(2,1)S(1)} %shard_map.86.refs_0_), channel_id=1, source_target_pairs={{8,0},{0,8},{24,16},{16,24},{9,1},{1,9},{25,17},{17,25},{10,2},{2,... | collective-permute-start | bytes 786440 | tf_op jit(solution)/shard_map/ppermute | solution.py:200
  26.7 22.7 %collective-permute-start.4 = (bf16[2,256,256]{2,1,0:T(8,128)(2,1)S(1)}, bf16[2,256,256]{2,1,0:T(8,128)(2,1)S(1)}, u32[]{:S(2)}, u32[]{:S(2)}) collective-permute-start(bf16[2,256,256]{2,1,0:T(8,128)(2,1)S(1)} %shard_map.86.refs_0_), channel_id=1, source_target_pairs={{0,0},{1,1},{2,2},{3,3},{4,16},{5,17},{6,18},{7,19},{8,8},{9,9},{1... | collective-permute-start | bytes 786440 | tf_op jit(solution)/shard_map/ppermute | solution.py:224
  53.3 1.9 %copy-start.25 = (bf16[256,256]{1,0:T(8,128)(2,1)S(1)}, bf16[256,256]{1,0:T(8,128)(2,1)}, u32[]{:S(2)}) copy-start(bf16[256,256]{1,0:T(8,128)(2,1)} %copy-done.24) | copy-start | bytes 393220
  53.3 9.8 %copy-start.9 = (bf16[2,256,256]{2,1,0:T(8,128)(2,1)S(1)}, bf16[2,256,256]{2,1,0:T(8,128)(2,1)}, u32[]{:S(2)}) copy-start(bf16[2,256,256]{2,1,0:T(8,128)(2,1)} %copy-done.8) | copy-start | bytes 786436
  53.3 9.8 %copy-start.15 = (bf16[2,256,256]{2,1,0:T(8,128)(2,1)S(1)}, bf16[2,256,256]{2,1,0:T(8,128)(2,1)}, u32[]{:S(2)}) copy-start(bf16[2,256,256]{2,1,0:T(8,128)(2,1)} %copy-done.14) | copy-start | bytes 786436
  53.4 9.8 %collective-permute-start.9 = (bf16[8,256,256]{2,1,0:T(8,128)(2,1)S(1)}, bf16[8,256,256]{2,1,0:T(8,128)(2,1)S(1)}, u32[]{:S(2)}, u32[]{:S(2)}) collective-permute-start(bf16[8,256,256]{2,1,0:T(8,128)(2,1)S(1)} %shard_map.88.own_ref), channel_id=1, source_target_pairs={{1,0},{0,1},{3,2},{2,3},{5,4},{4,5},{7,6},{6,7},{9,8},{8,9},{11,10... | collective-permute-start | bytes 3145736 | tf_op jit(solution)/shard_map/ppermute | solution.py:214
  55.2 7.9 %collective-permute-start.10 = (bf16[2,256,256]{2,1,0:T(8,128)(2,1)S(1)}, bf16[2,256,256]{2,1,0:T(8,128)(2,1)S(1)}, u32[]{:S(2)}, u32[]{:S(2)}) collective-permute-start(bf16[2,256,256]{2,1,0:T(8,128)(2,1)S(1)} %copy-done.11), channel_id=1, source_target_pairs={{16,0},{24,8},{0,16},{8,24},{17,1},{25,9},{1,17},{9,25},{18,2},{26... | collective-permute-start | bytes 786440 | tf_op jit(solution)/shard_map/ppermute | solution.py:200
  55.2 10.5 %collective-permute-start.8 = (bf16[256,256]{1,0:T(8,128)(2,1)S(1)}, bf16[256,256]{1,0:T(8,128)(2,1)S(1)}, u32[]{:S(2)}, u32[]{:S(2)}) collective-permute-start(bf16[256,256]{1,0:T(8,128)(2,1)S(1)} %copy-done.25), channel_id=1, source_target_pairs={{0,1},{1,0},{2,9},{3,8},{4,5},{5,4},{6,13},{7,12},{8,3},{9,2},{10,... | collective-permute-start | bytes 393224 | tf_op jit(solution)/shard_map/ppermute | solution.py:224
  55.3 10.4 %collective-permute-start.7 = (bf16[256,256]{1,0:T(8,128)(2,1)S(1)}, bf16[256,256]{1,0:T(8,128)(2,1)S(1)}, u32[]{:S(2)}, u32[]{:S(2)}) collective-permute-start(bf16[256,256]{1,0:T(8,128)(2,1)S(1)} %get-tuple-element.16.refs_1_), channel_id=1, source_target_pairs={{0,0},{1,1},{2,8},{3,9},{4,4},{5,5},{6,12},{7,13},{8,2},{9,3},{10,... | collective-permute-start | bytes 393224 | tf_op jit(solution)/shard_map/ppermute | solution.py:224
  68.1 7.3 %collective-permute-start.12 = (bf16[2,256,256]{2,1,0:T(8,128)(2,1)}, bf16[2,256,256]{2,1,0:T(8,128)(2,1)S(1)}, u32[]{:S(2)}, u32[]{:S(2)}) collective-permute-start(bf16[2,256,256]{2,1,0:T(8,128)(2,1)} %get-tuple-element.20.refs_0_), channel_id=1, source_target_pairs={{16,0},{24,8},{0,16},{8,24},{17,1},{25,9},{1,17},{9,25},{18,2},{26... | collective-permute-start | bytes 786440 | tf_op jit(solution)/shard_map/ppermute | solution.py:200
  68.4 7.4 %collective-permute-start.11 = (bf16[2,256,256]{2,1,0:T(8,128)(2,1)}, bf16[2,256,256]{2,1,0:T(8,128)(2,1)S(1)}, u32[]{:S(2)}, u32[]{:S(2)}) collective-permute-start(bf16[2,256,256]{2,1,0:T(8,128)(2,1)} %get-tuple-element.20.refs_0_), channel_id=1, source_target_pairs={{8,0},{0,8},{24,16},{16,24},{9,1},{1,9},{25,17},{17,25},{10,2},{2,... | collective-permute-start | bytes 786440 | tf_op jit(solution)/shard_map/ppermute | solution.py:200
  75.4 4.3 %collective-permute-start.13 = (bf16[1,256,256]{2,1,0:T(8,128)(2,1)S(1)}, bf16[1,256,256]{2,1,0:T(8,128)(2,1)S(1)}, u32[]{:S(2)}, u32[]{:S(2)}) collective-permute-start(bf16[1,256,256]{2,1,0:T(8,128)(2,1)S(1)} %slice.18), channel_id=1, source_target_pairs={{8,0},{0,8},{24,16},{16,24},{9,1},{1,9},{25,17},{17,25},{10,2},{2,... | collective-permute-start | bytes 393224 | tf_op jit(solution)/shard_map/ppermute | solution.py:200
  75.8 4.3 %collective-permute-start.14 = (bf16[1,256,256]{2,1,0:T(8,128)(2,1)S(1)}, bf16[1,256,256]{2,1,0:T(8,128)(2,1)S(1)}, u32[]{:S(2)}, u32[]{:S(2)}) collective-permute-start(bf16[1,256,256]{2,1,0:T(8,128)(2,1)S(1)} %slice.19), channel_id=1, source_target_pairs={{16,0},{24,8},{0,16},{8,24},{17,1},{25,9},{1,17},{9,25},{18,2},{26... | collective-permute-start | bytes 393224 | tf_op jit(solution)/shard_map/ppermute | solution.py:200
  81.7 5.7 %collective-permute-start.17 = (bf16[2,256,256]{2,1,0:T(8,128)(2,1)S(1)}, bf16[2,256,256]{2,1,0:T(8,128)(2,1)S(1)}, u32[]{:S(2)}, u32[]{:S(2)}) collective-permute-start(bf16[2,256,256]{2,1,0:T(8,128)(2,1)S(1)} %shard_map.91.refs_0_), channel_id=1, source_target_pairs={{16,0},{24,8},{0,16},{8,24},{17,1},{25,9},{1,17},{9,25},{18,2},{26... | collective-permute-start | bytes 786440 | tf_op jit(solution)/shard_map/ppermute | solution.py:200
  82.6 5.6 %collective-permute-start.16 = (bf16[2,256,256]{2,1,0:T(8,128)(2,1)S(1)}, bf16[2,256,256]{2,1,0:T(8,128)(2,1)S(1)}, u32[]{:S(2)}, u32[]{:S(2)}) collective-permute-start(bf16[2,256,256]{2,1,0:T(8,128)(2,1)S(1)} %shard_map.91.refs_0_), channel_id=1, source_target_pairs={{8,0},{0,8},{24,16},{16,24},{9,1},{1,9},{25,17},{17,25},{10,2},{2,... | collective-permute-start | bytes 786440 | tf_op jit(solution)/shard_map/ppermute | solution.py:200
  83.4 23.1 %collective-permute-start.15 = (bf16[2,256,256]{2,1,0:T(8,128)(2,1)S(1)}, bf16[2,256,256]{2,1,0:T(8,128)(2,1)S(1)}, u32[]{:S(2)}, u32[]{:S(2)}) collective-permute-start(bf16[2,256,256]{2,1,0:T(8,128)(2,1)S(1)} %shard_map.91.refs_0_), channel_id=1, source_target_pairs={{0,0},{1,1},{2,2},{3,3},{4,16},{5,17},{6,18},{7,19},{8,8},{9,9},{1... | collective-permute-start | bytes 786440 | tf_op jit(solution)/shard_map/ppermute | solution.py:224
  109.0 8.6 %copy-start.13 = (bf16[2,256,256]{2,1,0:T(8,128)(2,1)S(1)}, bf16[2,256,256]{2,1,0:T(8,128)(2,1)}, u32[]{:S(2)}) copy-start(bf16[2,256,256]{2,1,0:T(8,128)(2,1)} %copy-done.12) | copy-start | bytes 786436
  109.0 8.6 %collective-permute-start.20 = (bf16[8,256,256]{2,1,0:T(8,128)(2,1)S(1)}, bf16[8,256,256]{2,1,0:T(8,128)(2,1)S(1)}, u32[]{:S(2)}, u32[]{:S(2)}) collective-permute-start(bf16[8,256,256]{2,1,0:T(8,128)(2,1)S(1)} %shard_map.93.own_ref), channel_id=1, source_target_pairs={{1,0},{0,1},{3,2},{2,3},{5,4},{4,5},{7,6},{6,7},{9,8},{8,9},{11,10... | collective-permute-start | bytes 3145736 | tf_op jit(solution)/shard_map/ppermute | solution.py:214
  109.8 7.9 %collective-permute-start.21 = (bf16[2,256,256]{2,1,0:T(8,128)(2,1)S(1)}, bf16[2,256,256]{2,1,0:T(8,128)(2,1)S(1)}, u32[]{:S(2)}, u32[]{:S(2)}) collective-permute-start(bf16[2,256,256]{2,1,0:T(8,128)(2,1)S(1)} %collective-permute-done.16.refs_0_.refs_1_), channel_id=1, source_target_pairs={{16,0},{24,8},{0,16},{8,24},{17,1},{25,9},{1,17},{9,25},{18,2},{26... | collective-permute-start | bytes 786440 | tf_op jit(solution)/shard_map/ppermute | solution.py:200
  109.9 10.1 %collective-permute-start.19 = (bf16[256,256]{1,0:T(8,128)(2,1)S(1)}, bf16[256,256]{1,0:T(8,128)(2,1)S(1)}, u32[]{:S(2)}, u32[]{:S(2)}) collective-permute-start(bf16[256,256]{1,0:T(8,128)(2,1)S(1)} %copy-done.23), channel_id=1, source_target_pairs={{0,1},{1,0},{2,9},{3,8},{4,5},{5,4},{6,13},{7,12},{8,3},{9,2},{10,... | collective-permute-start | bytes 393224 | tf_op jit(solution)/shard_map/ppermute | solution.py:224
  109.9 10.1 %collective-permute-start.18 = (bf16[256,256]{1,0:T(8,128)(2,1)S(1)}, bf16[256,256]{1,0:T(8,128)(2,1)S(1)}, u32[]{:S(2)}, u32[]{:S(2)}) collective-permute-start(bf16[256,256]{1,0:T(8,128)(2,1)S(1)} %get-tuple-element.21.refs_1_), channel_id=1, source_target_pairs={{0,0},{1,1},{2,8},{3,9},{4,4},{5,5},{6,12},{7,13},{8,2},{9,3},{10,... | collective-permute-start | bytes 393224 | tf_op jit(solution)/shard_map/ppermute | solution.py:224
  (18 other events, 17.4 us)
Sparse Core Ops, SparseCore 0:
  8.9 29.4 all-gather.2
  68.2 28.9 all-gather.4
